TPU v7x, 512 devices: a whole 4x8x8 slice. The times are simulated.
512 devices in a mesh: shot: 64 (over x, z, y_lo), strip: 8 (over y_hi, core).
Axes of the slice: x: 4, y: 8 (y_hi: 4, y_lo: 2; y = y_hi * 2 + y_lo), z: 8, core: 2. Of those that a mesh axis runs over, the one named last changes fastest.
Arguments:
- source_field: bfloat16 [64, 16, 8, 16, 1024], P('shot', None, None, None, 'strip'), may hold values from -6 to 6
- receiver_field: bfloat16 [64, 16, 8, 16, 1024], P('shot', None, None, None, 'strip'), may hold values from -6 to 6
- shot_pos: int32 [64], P('shot'), may hold values from 0 to 1023
- offset_weight: int32 [33], replicated, may hold values from 1 to 16
Outputs:
- source_update: float32 [64, 16, 8, 16, 1024], P('shot', None, None, None, 'strip')
- receiver_update: float32 [64, 16, 8, 16, 1024], P('shot', None, None, None, 'strip')
All inputs are finite; a program needn't handle non-finite values.
Results may differ from a plain program's by a relative error of at most 0.0003.
Values may be sent and summed in bfloat16 or wider, within the bound.
A program may use at most 64 MiB of HBM per device.

v0:
```python
import jax
import jax.numpy as jnp
from jax import lax
from jax.sharding import PartitionSpec as P


def extended(cells, sides, width):
    for axis, dim in sides:
        count = lax.axis_size(axis)
        ends = count - 1
        head = lax.slice_in_dim(cells, 0, width, axis=dim)
        tail = lax.slice_in_dim(cells, cells.shape[dim] - width, cells.shape[dim], axis=dim)
        cells = jnp.concatenate(
            [
                lax.ppermute(tail, axis, [(i, (i + 1) % count) for i in range(ends)]),
                cells,
                lax.ppermute(head, axis, [((i + 1) % count, i) for i in range(ends)]),
            ],
            axis=dim,
        )
    return cells


def correlate(src_part, rec_rim, count, span):
    terms = [
        jnp.einsum(
            "stzyx,stzyx->zyx",
            src_part,
            rec_rim[..., k : k + span],
            preferred_element_type=jnp.float32,
        )
        for k in range(count)
    ]
    return jnp.stack(terms)


def local(source_field, receiver_field, shot_pos, offset_weight):
    width = source_field.shape[-1]
    steps = source_field.shape[1]
    strips = lax.axis_size("strip")
    nshot = source_field.shape[0] * lax.axis_size("shot")
    count = offset_weight.shape[0]
    reach = count // 2
    cells = lax.axis_index("strip") * width + jnp.arange(width, dtype=jnp.int32)
    apert = width * strips // 4
    inside = jnp.abs(cells[None, :] - shot_pos[:, None]) <= apert
    inside_full = inside[:, None, None, None, :]
    masked = jnp.where(inside_full, source_field, jnp.zeros_like(source_field))
    stacked = jnp.stack((receiver_field, masked))
    factor = offset_weight.astype(jnp.float32)[:, None, None, None] / float(nshot * steps)
    rims = extended(stacked, (("strip", 5),), reach)
    rec_rim = rims[0]
    src_rim = rims[1]
    partial_value = correlate(src_rim[..., reach : reach + width], rec_rim, count, width)
    image = lax.psum(partial_value, "shot")
    penalty_own = factor * image
    penalty_ext = extended(penalty_own, (("strip", 3),), reach)
    shape = source_field.shape
    src_upd = jnp.zeros(shape, jnp.float32)
    rec_upd = jnp.zeros(shape, jnp.float32)
    for k in range(count):
        src_upd = src_upd + penalty_own[k] * rec_rim[..., k : k + width].astype(jnp.float32)
        lower = 2 * reach - k
        rec_upd = rec_upd + penalty_ext[k][..., lower : lower + width] * src_rim[
            ..., lower : lower + width
        ].astype(jnp.float32)
    src_upd = jnp.where(inside_full, src_upd, jnp.zeros_like(src_upd))
    return (src_upd, rec_upd)


def solution(mesh):
    return jax.shard_map(
        local,
        mesh=mesh,
        in_specs=(
            P("shot", None, None, None, "strip"),
            P("shot", None, None, None, "strip"),
            P("shot"),
            P(),
        ),
        out_specs=(P("shot", None, None, None, "strip"), P("shot", None, None, None, "strip")),
        check_vma=False,
    )
```

profile of v0, /device:TPU:40, one launch (start us, length us, event | category | flops | bytes accessed | tf_op | source)
XLA Modules:
  0.0 747.6 jit_solution(437459324224031695)
XLA Ops:
  7.9 1.1 select_bitcast_fusion
  9.0 1.7 slice_maximum_fusion
  10.8 1.9 collective-permute-start
  12.7 5.8 collective-permute-start.1
  18.4 20.5 %collective-permute-done = bf16[2,1,16,8,16,16]{5,4,3,2,1,0:T(8,128)(2,1)S(1)} collective-permute-done((bf16[2,1,16,8,16,16]{5,4,3,2,1,0:T(8,128)(2,1)S(1)}, bf16[2,1,16,8,16,16]{5,4,3,2,1,0:T(8,128)(2,1)S(1)}, u32[]{:S(2)}, u32[]{:S(2)}) %collective-permute-start) | collective-permute-done | bytes 131104 | tf_op jit(solution)/shard_map/ppermute | solution.py:15
  38.9 2.9 collective-permute-done.1
  41.8 1.3 pad_maximum_fusion.1
  43.2 1.6 fusion.23
  44.9 1.6 fusion.14
  46.5 2.7 fusion.32
  50.4 0.6 constant_dynamic-update-slice_fusion.30
  55.4 0.6 constant_dynamic-update-slice_fusion.22
  57.3 0.6 constant_dynamic-update-slice_fusion.19
  58.5 0.6 constant_dynamic-update-slice_fusion.17
  64.7 0.6 constant_dynamic-update-slice_fusion.7
  67.2 0.6 constant_dynamic-update-slice_fusion.3
  68.5 0.6 constant_dynamic-update-slice_fusion.1
  69.8 605.0 %all-reduce.2.cloned.1.call-done = f32[33,8,16,128]{3,2,1,0:T(8,128)} async-done(((f32[33,8,16,128]{3,2,1,0:T(8,128)}), f32[33,8,16,128]{3,2,1,0:T(8,128)}) %all-reduce.2.cloned.1.call-update) | async-done | bytes 2162704 | tf_op jit(solution)/shard_map/psum | solution.py:55
  674.8 1.8 broadcast_multiply_fusion
  676.6 0.9 slice_bitcast_fusion.66
  677.5 1.1 slice_bitcast_fusion.67
  678.6 2.9 fusion.33
  681.5 2.5 copy.6
  684.0 3.3 copy.7
  687.3 1.9 collective-permute-start.3
  689.2 2.6 collective-permute-start.2
  691.8 8.4 %add_select_fusion = f32[1,16,8,16,128]{4,3,2,1,0:T(8,128)} fusion(f32[8,16,128]{2,1,0:T(8,128)} %get-tuple-element.71, f32[8,16,128]{2,1,0:T(8,128)} %get-tuple-element.72, f32[8,16,128]{2,1,0:T(8,128)} %get-tuple-element.73, f32[8,16,128]{2,1,0:T(8,128)} %get-tuple-element.74, f32[8,16,128]{2,1,0:T(8,128)} %get-tuple-element.75, ...), kind=kLoop, calls=%fused_computation.74 | loop fusion | flops 25952256 | bytes 20512896 | tf_op jit(solution)/shard_map/jit(_where)/select_n | solution.py:67
  700.2 18.7 %collective-permute-done.2 = f32[33,8,16,16]{0,3,2,1:T(8,128)} collective-permute-done((f32[33,8,16,16]{0,3,2,1:T(8,128)S(1)}, f32[33,8,16,16]{0,3,2,1:T(8,128)}, u32[]{:S(2)}, u32[]{:S(2)}) %collective-permute-start.2) | collective-permute-done | bytes 270368 | tf_op jit(solution)/shard_map/ppermute | solution.py:15
  718.8 3.8 copy.8
  722.6 3.9 copy.9
  726.6 4.0 pad_maximum_fusion
  733.8 7.0 multiply_add_fusion
  (75 shorter events, 19.5 us)
Async XLA Ops:
  7.2 34.6 %copy-start.2 = (bf16[1,16,8,16,128]{4,3,2,1,0:T(8,128)(2,1)S(1)}, bf16[1,16,8,16,128]{4,3,2,1,0:T(8,128)(2,1)}, u32[]{:S(2)}) copy-start(bf16[1,16,8,16,128]{4,3,2,1,0:T(8,128)(2,1)} %param.5) | copy-start | bytes 1572868
  7.2 667.6 %all-reduce.2.cloned.1.call-start = ((), (), s32[]{:S(2)}) async-start(), calls=%async_computation | async-start | bytes 4325376 | tf_op jit(solution)/shard_map/psum | solution.py:55
  10.8 28.2 %collective-permute-start = (bf16[2,1,16,8,16,16]{5,4,3,2,1,0:T(8,128)(2,1)S(1)}, bf16[2,1,16,8,16,16]{5,4,3,2,1,0:T(8,128)(2,1)S(1)}, u32[]{:S(2)}, u32[]{:S(2)}) collective-permute-start(bf16[2,1,16,8,16,16]{5,4,3,2,1,0:T(8,128)(2,1)S(1)} %get-tuple-element.111), channel_id=1, source_target_pairs={{0,1},{1,2},{2,3},{3,4},{4,5},{5,6},{6,7},{8,9},{9,10},{10,11},{11... | collective-permute-start | bytes 393224 | tf_op jit(solution)/shard_map/ppermute | solution.py:15
  12.7 29.1 %collective-permute-start.1 = (bf16[2,1,16,8,16,16]{5,4,3,2,1,0:T(8,128)(2,1)S(1)}, bf16[2,1,16,8,16,16]{5,4,3,2,1,0:T(8,128)(2,1)S(1)}, u32[]{:S(2)}, u32[]{:S(2)}) collective-permute-start(bf16[2,1,16,8,16,16]{5,4,3,2,1,0:T(8,128)(2,1)S(1)} %get-tuple-element.112), channel_id=1, source_target_pairs={{1,0},{2,1},{3,2},{4,3},{5,4},{6,5},{7,6},{9,8},{10,9},{11,10},{12... | collective-permute-start | bytes 393224 | tf_op jit(solution)/shard_map/ppermute | solution.py:17
  59.8 10.0 %copy-start.3 = (s32[33]{0:T(128)S(1)}, s32[33]{0:T(128)}, u32[]{:S(2)}) copy-start(s32[33]{0:T(128)} %param.7) | copy-start | bytes 400
  676.6 2.0 copy-start
  687.3 35.3 %collective-permute-start.3 = (f32[33,8,16,16]{0,3,2,1:T(8,128)}, f32[33,8,16,16]{0,3,2,1:T(8,128)}, u32[]{:S(2)}, u32[]{:S(2)}) collective-permute-start(f32[33,8,16,16]{0,3,2,1:T(8,128)} %copy.7), channel_id=1, source_target_pairs={{1,0},{2,1},{3,2},{4,3},{5,4},{6,5},{7,6},{9,8},{10,9},{11,10},{12... | collective-permute-start | bytes 811016 | tf_op jit(solution)/shard_map/ppermute | solution.py:17
  689.2 29.6 %collective-permute-start.2 = (f32[33,8,16,16]{0,3,2,1:T(8,128)S(1)}, f32[33,8,16,16]{0,3,2,1:T(8,128)}, u32[]{:S(2)}, u32[]{:S(2)}) collective-permute-start(f32[33,8,16,16]{0,3,2,1:T(8,128)S(1)} %copy.6), channel_id=1, source_target_pairs={{0,1},{1,2},{2,3},{3,4},{4,5},{5,6},{6,7},{8,9},{9,10},{10,11},{11... | collective-permute-start | bytes 811016 | tf_op jit(solution)/shard_map/ppermute | solution.py:15
  722.6 4.0 copy-start.1
Sparse Core Ops, SparseCore 0:
  69.9 604.8 all-reduce.1
where the time goes:
time: 748 us
  waiting for transfers between devices  647 us (86%)
  local copies, waits for them, and re-layouts  42.3 us (6%)
  other arithmetic  31.2 us (4%)
  between operations  14.9 us (2%)
  starting transfers between devices  12.2 us (2%)
    psum x1, waiting for transfers between devices, local(): image = lax.psum(partial_value, 'shot')  605 us
    ppermute x2, waiting for transfers between devices, extended(): lax.ppermute(tail, axis, [(i, (i + 1) % count) for i in range(ends)])  39.2 us
    unnamed x40, local copies, waits for them, and re-layouts  19.9 us
  transfers between devices with their start and end apart: 5, of which 4 were waited for; matrix products, arithmetic and copies ran while one was open for 2% of the time, Pallas kernels for 0%

commit v1 on v0

v1 whole, which is shorter than its diff:
```python
import functools

import jax
import jax.numpy as jnp
from jax import lax
from jax.experimental import pallas as pl
from jax.experimental.pallas import tpu as pltpu
from jax.sharding import PartitionSpec as P

MESH = pl.DeviceIdType.MESH
VMEM = pl.BlockSpec(memory_space=pltpu.VMEM)
SMEM = pl.BlockSpec(memory_space=pltpu.SMEM)
F32 = jnp.float32

NUM_X, NUM_Z, NUM_Y = 4, 8, 2
ROWS = 8
PAD = 36
QUARTER = PAD // 4
params = functools.partial(pltpu.CompilerParams, vmem_limit_bytes=56 * 2**20)


def prepare_kernel(strips, shots_pos, rec, src, rec_ext, src_ext, send, recv):
    steps, width = rec.shape[0], rec.shape[-1]
    rim = (rec_ext.shape[1] - width) // 2
    strip = lax.axis_index("strip")
    left, right = lax.rem(strip + strips - 1, strips), lax.rem(strip + 1, strips)
    barrier = pltpu.get_barrier_semaphore()
    for other in (left, right):
        pl.semaphore_signal(barrier, inc=1, device_id={"strip": other}, device_id_type=MESH)
    pos = shots_pos[0]
    cells = strip * width + lax.broadcasted_iota(jnp.int32, (width, width), 0)
    inside = jnp.abs(cells - pos) <= width * strips // 4

    @pl.loop(0, steps)
    def _(t):
        r = rec[t].reshape(width, width).astype(F32).T
        rec_ext[t, rim : rim + width] = r.astype(jnp.bfloat16)
        s = src[t].reshape(width, width).astype(F32).T
        src_ext[t, rim : rim + width] = jnp.where(inside, s, 0.0).astype(jnp.bfloat16)

    pl.semaphore_wait(barrier, 2)
    copies = []
    for i, ext in enumerate((rec_ext, src_ext)):
        copies.append(
            pltpu.make_async_remote_copy(
                src_ref=ext.at[:, width : width + rim],
                dst_ref=ext.at[:, 0:rim],
                send_sem=send.at[2 * i],
                recv_sem=recv.at[2 * i],
                device_id={"strip": right},
                device_id_type=MESH,
            )
        )
        copies.append(
            pltpu.make_async_remote_copy(
                src_ref=ext.at[:, rim : 2 * rim],
                dst_ref=ext.at[:, rim + width : 2 * rim + width],
                send_sem=send.at[2 * i + 1],
                recv_sem=recv.at[2 * i + 1],
                device_id={"strip": left},
                device_id_type=MESH,
            )
        )
    for copy in copies:
        copy.start()
    for copy in copies:
        copy.wait()
    has_left = jnp.full((rim, width), strip, jnp.int32) > 0
    has_right = jnp.full((rim, width), strip, jnp.int32) < strips - 1

    @pl.loop(0, steps)
    def _(t):
        for ext in (rec_ext, src_ext):
            low = ext[t, 0:rim].astype(F32)
            ext[t, 0:rim] = jnp.where(has_left, low, 0.0).astype(jnp.bfloat16)
            high = ext[t, rim + width : 2 * rim + width].astype(F32)
            ext[t, rim + width : 2 * rim + width] = jnp.where(has_right, high, 0.0).astype(jnp.bfloat16)


def image_kernel(terms, weight, rec_ext, src_ext, image, rec32, src32):
    steps, span, lanes = rec_ext.shape
    count = weight.shape[0]
    rim = count // 2

    @pl.loop(0, steps)
    def _(t):
        rec32[t] = rec_ext[t].astype(F32)
        src32[t] = src_ext[t].astype(F32)

    scale = [weight[k].astype(F32) * (1.0 / terms) for k in range(count)]

    @pl.loop(0, image.shape[0])
    def _(g):
        base = pl.multiple_of(g * ROWS, ROWS)
        own = [src32[t, pl.ds(base + rim, ROWS)] for t in range(steps)]
        for k in range(count):
            total = own[0] * rec32[0, pl.ds(base + k, ROWS)]
            for t in range(1, steps):
                total += own[t] * rec32[t, pl.ds(base + k, ROWS)]
            image[g, k] = total * scale[k]
        for k in range(count, PAD):
            image[g, k] = jnp.zeros((ROWS, lanes), F32)


def ring_chains(n):
    return ((1, n // 2, 0), (-1, n // 2 - 1, 0), (-1, n // 2, 1), (1, n // 2 - 1, 1))


def reduce_kernel(strips, count, img, out, slot_a, slot_b, acc_a, acc_b, in_a, in_b, in_y, fin, send, recv):
    shot, strip = lax.axis_index("shot"), lax.axis_index("strip")
    x, z, y = shot // (NUM_Z * NUM_Y), shot // NUM_Y % NUM_Z, shot % NUM_Y
    half_k = PAD // 2

    def at_x(i):
        return {"shot": (i * NUM_Z + z) * NUM_Y + y}

    def at_z(i):
        return {"shot": (x * NUM_Z + i) * NUM_Y + y}

    def wrap(i, n):
        return lax.rem(i + n, n)

    pair = {"shot": shot + 1 - 2 * y}
    left, right = {"strip": wrap(strip - 1, strips)}, {"strip": wrap(strip + 1, strips)}
    others = [at_x(wrap(x + d, NUM_X)) for d in range(1, NUM_X)]
    others += [at_z(wrap(z + d, NUM_Z)) for d in range(1, NUM_Z)]
    others += [pair, left, right]
    barrier = pltpu.get_barrier_semaphore()
    for other in others:
        pl.semaphore_signal(barrier, inc=1, device_id=other, device_id_type=MESH)
    pl.semaphore_wait(barrier, len(others))

    started = []

    def push(src_ref, dst_ref, device):
        i = len(started)
        copy = pltpu.make_async_remote_copy(
            src_ref=src_ref,
            dst_ref=dst_ref,
            send_sem=send.at[i],
            recv_sem=recv.at[i],
            device_id=device,
            device_id_type=MESH,
        )
        copy.start()
        started.append(copy)
        return copy

    def group_a(i):
        return i + (i // (NUM_Z // 2)) * 2 * NUM_X

    def group_b(i, half):
        return NUM_Z // 2 + 2 * i + half

    def part_a(ref, owner, half):
        return ref.at[group_a(owner), pl.ds(half * half_k, half_k)]

    def part_b(ref, owner, half):
        return ref.at[group_b(owner, half)]

    plans = {
        "a": (NUM_Z, z, at_z, part_a, slot_a),
        "b": (NUM_X, x, at_x, part_b, slot_b),
    }
    arrived = {}
    slots = {}
    for name, (n, *_) in plans.items():
        first = 0
        for c, (_, hops, _) in enumerate(ring_chains(n)):
            slots[name, c] = first
            first += hops

    def reduce_step(name, j):
        n, here, device, part, slot = plans[name]
        for c, (way, hops, half) in enumerate(ring_chains(n)):
            if j > hops:
                continue
            owner = wrap(here + way * (hops + 1 - j), n)
            mine = part(img, owner, half)
            if j > 1:
                held = slot.at[slots[name, c] + j - 2]
                arrived[name, c].wait_recv()
                held[...] += mine[...]
                mine = held
            arrived[name, c] = push(mine, slot.at[slots[name, c] + j - 1], device(wrap(here + way, n)))

    def reduce_end(name, store):
        n, here, _, part, slot = plans[name]
        chains = ring_chains(n)
        for half in range(2):
            total = part(img, here, half)[...]
            for c, (_, hops, side) in enumerate(chains):
                if side == half:
                    arrived[name, c].wait_recv()
                    total += slot[slots[name, c] + hops - 1]
            store(half, total)

    def store_a(half, total):
        acc_a[half * half_k : (half + 1) * half_k] = total

    def store_b(half, total):
        acc_b[half] = total

    def piece_b(ref, i):
        return ref.at[i // 4, pl.ds(i % 4 * QUARTER, QUARTER)]

    reduce_step("a", 1)
    reduce_step("b", 1)
    reduce_step("a", 2)
    reduce_step("b", 2)
    reduce_end("b", store_b)
    second_b = []
    for d in range(1, NUM_Z):
        other = wrap(z + d, NUM_Z)
        second_b.append(push(piece_b(acc_b, other), in_b.at[d - 1], at_z(other)))
    reduce_step("a", 3)
    reduce_step("a", 4)
    reduce_end("a", store_a)
    second_a = []
    for d in range(1, NUM_X):
        other = wrap(x + d, NUM_X)
        second_a.append(push(acc_a.at[pl.ds(other * QUARTER, QUARTER)], in_a.at[d - 1], at_x(other)))

    total = piece_b(acc_b, z)[...]
    for d in range(1, NUM_Z):
        second_b[d - 1].wait_recv()
        total += in_b[d - 1]
    fin[1] = total
    pair_b = push(fin.at[1], in_y.at[1], pair)
    total = acc_a[pl.ds(x * QUARTER, QUARTER)]
    for d in range(1, NUM_X):
        second_a[d - 1].wait_recv()
        total += in_a[d - 1]
    fin[0] = total
    pair_a = push(fin.at[0], in_y.at[0], pair)

    mine_b = out.at[group_b(x, z // 4), pl.ds(z % 4 * QUARTER, QUARTER)]
    pair_b.wait_recv()
    mine_b[...] = fin[1] + in_y[1]
    third_b = [push(mine_b, mine_b, at_z(wrap(z + d, NUM_Z))) for d in range(1, NUM_Z)]
    mine_a = out.at[group_a(z), pl.ds(x * QUARTER, QUARTER)]
    pair_a.wait_recv()
    mine_a[...] = fin[0] + in_y[0]
    third_a = [push(mine_a, mine_a, at_x(wrap(x + d, NUM_X))) for d in range(1, NUM_X)]

    def gather_step(name, j):
        n, here, device, part, _ = plans[name]
        for c, (way, hops, half) in enumerate(ring_chains(n)):
            if j > hops + 1:
                continue
            if j > 1:
                arrived[name, c].wait_recv()
            if j <= hops:
                held = part(out, wrap(here - way * (j - 1), n), half)
                arrived[name, c] = push(held, held, device(wrap(here + way, n)))

    for copy in third_b:
        copy.wait_recv()
    gather_step("b", 1)
    for copy in third_a:
        copy.wait_recv()
    gather_step("a", 1)
    gather_step("b", 2)
    gather_step("a", 2)
    gather_step("b", 3)
    gather_step("a", 3)
    gather_step("a", 4)
    gather_step("a", 5)

    rim = count // 2
    groups = img.shape[0]
    edge = rim // ROWS
    to_right = push(
        out.at[pl.ds(groups - edge, edge), pl.ds(rim + 1, rim)],
        out.at[pl.ds(groups, edge), pl.ds(rim + 1, rim)],
        right,
    )
    to_left = push(out.at[pl.ds(0, edge), pl.ds(0, rim)], out.at[pl.ds(groups + edge, edge), pl.ds(0, rim)], left)
    to_right.wait_recv()
    to_left.wait_recv()
    for copy in started:
        copy.wait_send()


def update_kernel(strips, shots_pos, rec_ext, src_ext, penalty, src_upd, rec_upd, rec32, src32, pen, held):
    steps, span, lanes = rec_ext.shape
    width = lanes
    rim = (span - width) // 2
    count = 2 * rim + 1
    groups = width // ROWS
    edge = rim // ROWS
    strip = lax.axis_index("strip")
    pos = shots_pos[0]

    @pl.loop(0, steps)
    def _(t):
        rec32[t] = rec_ext[t].astype(F32)
        src32[t] = src_ext[t].astype(F32)

    @pl.loop(0, count)
    def _(k):
        for g in range(groups):
            pen[k, rim + g * ROWS : rim + (g + 1) * ROWS] = penalty[g, k]
        for g in range(edge):
            pen[k, g * ROWS : (g + 1) * ROWS] = penalty[groups + g, k]
            start = rim + width + g * ROWS
            pen[k, start : start + ROWS] = penalty[groups + edge + g, k]

    @pl.loop(0, groups)
    def _(g):
        base = pl.multiple_of(g * ROWS, ROWS)
        cells = strip * width + base + lax.broadcasted_iota(jnp.int32, (ROWS, lanes), 0)
        inside = jnp.abs(cells - pos) <= width * strips // 4
        total = [jnp.zeros((ROWS, lanes), F32)] * steps
        for k in range(count):
            p = pen[k, pl.ds(base + rim, ROWS)]
            total = [total[t] + p * rec32[t, pl.ds(base + k, ROWS)] for t in range(steps)]
        for t in range(steps):
            held[t, pl.ds(base, ROWS)] = jnp.where(inside, total[t], 0.0)

    @pl.loop(0, steps)
    def _(t):
        src_upd[t] = held[t].T.reshape(src_upd.shape[1:])

    @pl.loop(0, groups)
    def _(g):
        base = pl.multiple_of(g * ROWS, ROWS)
        total = [jnp.zeros((ROWS, lanes), F32)] * steps
        for k in range(count):
            low = base + 2 * rim - k
            p = pen[k, pl.ds(low, ROWS)]
            total = [total[t] + p * src32[t, pl.ds(low, ROWS)] for t in range(steps)]
        for t in range(steps):
            held[t, pl.ds(base, ROWS)] = total[t]

    @pl.loop(0, steps)
    def _(t):
        rec_upd[t] = held[t].T.reshape(rec_upd.shape[1:])


def reduce_call(strips, count, image):
    groups, _, _, width = image.shape
    rim = count // 2
    quarter = (QUARTER, ROWS, width)
    return pl.pallas_call(
        functools.partial(reduce_kernel, strips, count),
        out_shape=jax.ShapeDtypeStruct((groups + 2 * rim // ROWS, PAD, ROWS, width), F32),
        in_specs=[VMEM],
        out_specs=VMEM,
        scratch_shapes=[
            pltpu.VMEM((2 * NUM_Z - 2, PAD // 2, ROWS, width), F32),
            pltpu.VMEM((2 * NUM_X - 2, PAD, ROWS, width), F32),
            pltpu.VMEM((PAD, ROWS, width), F32),
            pltpu.VMEM((2, PAD, ROWS, width), F32),
            pltpu.VMEM((NUM_X - 1,) + quarter, F32),
            pltpu.VMEM((NUM_Z - 1,) + quarter, F32),
            pltpu.VMEM((2,) + quarter, F32),
            pltpu.VMEM((2,) + quarter, F32),
            pltpu.SemaphoreType.DMA((64,)),
            pltpu.SemaphoreType.DMA((64,)),
        ],
        compiler_params=params(collective_id=1, has_side_effects=True),
        name="reduce",
    )(image)


def local(strips, shots, source_field, receiver_field, shot_pos, offset_weight):
    src, rec = source_field[0], receiver_field[0]
    steps, depth, lateral, width = src.shape
    count = offset_weight.shape[0]
    rim = count // 2
    span = width + 2 * rim
    groups = width // ROWS

    ext = jax.ShapeDtypeStruct((steps, span, width), jnp.bfloat16)
    rec_ext, src_ext = pl.pallas_call(
        functools.partial(prepare_kernel, strips),
        out_shape=(ext, ext),
        in_specs=[SMEM, VMEM, VMEM],
        out_specs=(VMEM, VMEM),
        scratch_shapes=[pltpu.SemaphoreType.DMA((4,)), pltpu.SemaphoreType.DMA((4,))],
        compiler_params=params(collective_id=0, has_side_effects=True),
        name="prepare",
    )(shot_pos, rec, src)

    wide = pltpu.VMEM((steps, span, width), F32)
    image = pl.pallas_call(
        functools.partial(image_kernel, float(shots * steps)),
        out_shape=jax.ShapeDtypeStruct((groups, PAD, ROWS, width), F32),
        in_specs=[SMEM, VMEM, VMEM],
        out_specs=VMEM,
        scratch_shapes=[wide, wide],
        compiler_params=params(),
        name="image",
    )(offset_weight, rec_ext, src_ext)

    penalty = reduce_call(strips, count, image)

    upd = jax.ShapeDtypeStruct(src.shape, F32)
    src_upd, rec_upd = pl.pallas_call(
        functools.partial(update_kernel, strips),
        out_shape=(upd, upd),
        in_specs=[SMEM, VMEM, VMEM, VMEM],
        out_specs=(VMEM, VMEM),
        scratch_shapes=[
            wide,
            wide,
            pltpu.VMEM((count, span, width), F32),
            pltpu.VMEM((steps, width, width), F32),
        ],
        compiler_params=params(),
        name="update",
    )(shot_pos, rec_ext, src_ext, penalty)
    return src_upd[None], rec_upd[None]


def solution(mesh):
    return jax.shard_map(
        functools.partial(local, mesh.shape["strip"], mesh.shape["shot"]),
        mesh=mesh,
        in_specs=(
            P("shot", None, None, None, "strip"),
            P("shot", None, None, None, "strip"),
            P("shot"),
            P(),
        ),
        out_specs=(P("shot", None, None, None, "strip"), P("shot", None, None, None, "strip")),
        check_vma=False,
    )
```

time: 748 us -> 116 us (0.16)
  the two profiles are of different devices: /device:TPU:40 before, /device:TPU:1 now
where the time goes in v1:
time: 116 us
  Pallas kernels  115 us (99%)
  between operations  1.29 us (1%)
    pallas_call x1, Pallas kernels, reduce_call(): pl.pallas_call(functools.partial(reduce_kernel, strips, count), out_shape...  81.4 us
    pallas_call x1, Pallas kernels, local(): pl.pallas_call(functools.partial(update_kernel, strips), out_shape=(upd,...  13.1 us
    pallas_call x1, Pallas kernels, local(): pl.pallas_call(functools.partial(prepare_kernel, strips), out_shape=(ext,...  12.6 us
    pallas_call x1, Pallas kernels, local(): pl.pallas_call(functools.partial(image_kernel, float(shots * steps)), out...  7.68 us

profile of v1, /device:TPU:1, one launch (start us, length us, event | category | flops | bytes accessed | tf_op | source)
XLA Modules:
  0.0 116.1 jit_solution(5778555135674115697)
XLA Ops:
  1.3 12.6 %prepare.1 = (bf16[16,160,128]{2,1,0:T(8,128)(2,1)}, bf16[16,160,128]{2,1,0:T(8,128)(2,1)}) custom-call(s32[1]{0:T(128)S(6)} %copy.6.shots_pos, bf16[16,8,16,128]{3,2,1,0:T(8,128)(2,1)} %bitcast.4, bf16[16,8,16,128]{3,2,1,0:T(8,128)(2,1)} %bitcast.5), custom_call_target="tpu_custom_call" | custom-call | tf_op jit(solution)/shard_map/prepare/pallas_call | solution.py:376
  13.9 7.7 %image.1.img = f32[16,36,8,128]{3,2,1,0:T(8,128)} custom-call(s32[33]{0:T(128)} %weight.1, bf16[16,160,128]{2,1,0:T(8,128)(2,1)} %get-tuple-element.6.rec_ext, bf16[16,160,128]{2,1,0:T(8,128)(2,1)} %get-tuple-element.7.src_ext), custom_call_target="tpu_custom_call" | custom-call | tf_op jit(solution)/shard_map/image/pallas_call | solution.py:387
  21.6 81.4 %reduce.1.penalty = f32[20,36,8,128]{3,2,1,0:T(8,128)} custom-call(f32[16,36,8,128]{3,2,1,0:T(8,128)} %image.1.img), custom_call_target="tpu_custom_call" | custom-call | tf_op jit(solution)/shard_map/reduce/pallas_call | solution.py:345
  103.0 13.1 %update.1 = (f32[16,8,16,128]{3,2,1,0:T(8,128)}, f32[16,8,16,128]{3,2,1,0:T(8,128)}) custom-call(s32[1]{0:T(128)S(6)} %copy.6.shots_pos, bf16[16,160,128]{2,1,0:T(8,128)(2,1)} %get-tuple-element.6.rec_ext, bf16[16,160,128]{2,1,0:T(8,128)(2,1)} %get-tuple-element.7.src_ext, f32[20,36,8,128]{3,2,1,0:T(8,128)} %reduce.1.penalty), custom_call_target="tpu_custom_call" | custom-call | tf_op jit(solution)/shard_map/update/pallas_call | solution.py:400

commit v2 on v0

v2 whole, which is shorter than its diff:
```python
import functools

import jax
import jax.numpy as jnp
from jax import lax
from jax.experimental import pallas as pl
from jax.experimental.pallas import tpu as pltpu
from jax.sharding import PartitionSpec as P

MESH = pl.DeviceIdType.MESH
VMEM = pl.BlockSpec(memory_space=pltpu.VMEM)
SMEM = pl.BlockSpec(memory_space=pltpu.SMEM)
F32 = jnp.float32

NUM_X, NUM_Z, NUM_Y = 4, 8, 2
ROWS = 8
BATCH, SOME = 4, 8
PAD = 36
QUARTER = PAD // 4
WORDS = (QUARTER + 1) // 2
TINY, LIMIT, STEPS_2 = 1e-30, 32767.0, 16.0


def unit_matrix(rows, columns):
    i = lax.broadcasted_iota(jnp.int32, (rows, columns), 0)
    j = lax.broadcasted_iota(jnp.int32, (rows, columns), 1)
    return jnp.where(lax.rem(j, rows) == i, 1.0, 0.0).astype(jnp.bfloat16)


def turned(unit, values):
    return lax.dot_general(unit, values, (((1,), (1,)), ((), ())), preferred_element_type=F32)


def turned_pair(unit, values):
    high = values.astype(jnp.bfloat16)
    low = (values - high.astype(F32)).astype(jnp.bfloat16)
    return turned(unit, jnp.concatenate([high, low], axis=1))


def encode(values):
    top = jnp.maximum(jnp.max(jnp.abs(values), axis=0), TINY)
    code = jnp.ceil(jnp.log2(top) * STEPS_2)
    scaled = jnp.round(values * (LIMIT / jnp.exp2(code * (1.0 / STEPS_2))))
    whole = jnp.clip(scaled, -LIMIT, LIMIT).astype(jnp.int32)
    low = jnp.concatenate([whole[WORDS:], code.astype(jnp.int32)[None]])
    return (whole[:WORDS] << 16) | (low & 0xFFFF)


def decode(words):
    high, low = words >> 16, (words << 16) >> 16
    scale = jnp.exp2(low[WORDS - 1].astype(F32) * (1.0 / STEPS_2)) * (1.0 / LIMIT)
    return jnp.concatenate([high, low[: WORDS - 1]]).astype(F32) * scale


def ring_chains(n):
    return ((1, n // 2, 0), (-1, n // 2 - 1, 0), (-1, n // 2, 1), (1, n // 2 - 1, 1))


def fused_kernel(
    strips,
    terms_count,
    shots_pos,
    weight,
    rec,
    src,
    src_upd,
    rec_upd,
    rec32,
    src32,
    edge_out,
    edge_in,
    img,
    out,
    pen,
    held,
    stage_z,
    stage_x,
    slot_z,
    slot_x,
    send_z,
    send_x,
    in_z,
    in_x,
    pair_out,
    pair_in,
    send,
    recv,
):
    steps, width = rec.shape[0], rec.shape[-1]
    count = weight.shape[0]
    rim = count // 2
    edge = rim // ROWS
    groups = width // ROWS
    shot, strip = lax.axis_index("shot"), lax.axis_index("strip")
    x, z, y = shot // (NUM_Z * NUM_Y), shot // NUM_Y % NUM_Z, shot % NUM_Y

    def at_x(i):
        return {"shot": (i * NUM_Z + z) * NUM_Y + y}

    def at_z(i):
        return {"shot": (x * NUM_Z + i) * NUM_Y + y}

    def wrap(i, n):
        return lax.rem(i + n, n)

    pair = {"shot": shot + 1 - 2 * y}
    left, right = {"strip": wrap(strip - 1, strips)}, {"strip": wrap(strip + 1, strips)}
    others = [at_x(wrap(x + d, NUM_X)) for d in range(1, NUM_X)]
    others += [at_z(wrap(z + d, NUM_Z)) for d in range(1, NUM_Z)]
    others += [pair, left, right]
    barrier = pltpu.get_barrier_semaphore()
    for other in others:
        pl.semaphore_signal(barrier, inc=1, device_id=other, device_id_type=MESH)

    def group_z(i):
        return NUM_Z // 2 + i

    def group_x(i, half):
        return 2 * i + half + i // (NUM_X // 2) * NUM_Z

    def own(name, owner, half):
        if name == "z":
            return [(group_z(owner), half * 2 + q) for q in range(2)]
        return [(group_x(owner, half), q) for q in range(4)]

    def terms(place):
        group, q = place
        return img[group, q * QUARTER : (q + 1) * QUARTER]

    plans = {
        "z": (NUM_Z, z, at_z, stage_z, slot_z),
        "x": (NUM_X, x, at_x, stage_x, slot_x),
    }
    arrived = {}
    slots = {}
    for name, (n, *_) in plans.items():
        first = 0
        for c, (_, hops, _) in enumerate(ring_chains(n)):
            slots[name, c] = first
            first += hops
    started = []

    def push(src_ref, dst_ref, device):
        i = len(started)
        copy = pltpu.make_async_remote_copy(
            src_ref=src_ref,
            dst_ref=dst_ref,
            send_sem=send.at[i],
            recv_sem=recv.at[i],
            device_id=device,
            device_id_type=MESH,
        )
        copy.start()
        started.append(copy)
        return copy

    def fill(name, c):
        n, here, _, stage, _ = plans[name]
        way, hops, half = ring_chains(n)[c]
        for q, place in enumerate(own(name, wrap(here + way * hops, n), half)):
            stage[c, q] = encode(terms(place))

    def reduce_step(name, j, c):
        n, here, device, stage, slot = plans[name]
        way, hops, half = ring_chains(n)[c]
        if j > hops:
            return
        held = stage.at[c]
        if j > 1:
            held = slot.at[slots[name, c] + j - 2]
            arrived[name, c].wait_recv()
            for q, place in enumerate(own(name, wrap(here + way * (hops + 1 - j), n), half)):
                held[q] = encode(decode(held[q]) + terms(place))
        arrived[name, c] = push(held, slot.at[slots[name, c] + j - 1], device(wrap(here + way, n)))

    def reduce_end(name, half, q):
        n, here, _, _, slot = plans[name]
        total = terms(own(name, here, half)[q])
        for c, (_, hops, side) in enumerate(ring_chains(n)):
            if side == half:
                total += decode(slot[slots[name, c] + hops - 1, q])
        return total

    unit = unit_matrix(width, width)
    pos = shots_pos[0]

    def inside(first, rows):
        cells = strip * width + first + lax.broadcasted_iota(jnp.int32, (rows, width), 0)
        return jnp.abs(cells - pos) <= width * strips // 4

    def take_in(field, wide, which, mask):
        for t in range(steps):
            value = turned(unit, field[t].reshape(width, width))
            if mask is not None:
                value = jnp.where(mask, value, 0.0)
            wide[t, rim : rim + width] = value
            edge_out[which, 0, t] = value[width - rim :].astype(jnp.bfloat16)
            edge_out[which, 1, t] = value[:rim].astype(jnp.bfloat16)

    def push_edges(which):
        return [push(edge_out.at[which, side], edge_in.at[which, side], (right, left)[side]) for side in range(2)]

    def take_edges(copies, wide, which):
        for copy in copies:
            copy.wait_recv()
        has_left = jnp.full((rim, width), strip, jnp.int32) > 0
        has_right = jnp.full((rim, width), strip, jnp.int32) < strips - 1
        for t in range(steps):
            wide[t, 0:rim] = jnp.where(has_left, edge_in[which, 0, t].astype(F32), 0.0)
            wide[t, rim + width : 2 * rim + width] = jnp.where(has_right, edge_in[which, 1, t].astype(F32), 0.0)

    take_in(rec, rec32, 0, None)
    pl.semaphore_wait(barrier, len(others))
    rec_edges = push_edges(0)
    take_in(src, src32, 1, inside(0, width))
    src_edges = push_edges(1)

    scale = [weight[k].astype(F32) * (1.0 / terms_count) for k in range(count)]
    spread = count + (BATCH - 1) * ROWS

    def uses(low):
        return [(g, low - g * ROWS) for g in range(BATCH) if 0 <= low - g * ROWS < count]

    def correlate(i):
        base = pl.multiple_of(i * BATCH * ROWS, ROWS)
        for first in range(0, steps, SOME):
            mine = [
                [src32[first + t, pl.ds(base + g * ROWS + rim, ROWS)] for t in range(SOME)] for g in range(BATCH)
            ]
            for low in range(spread):
                window = [rec32[first + t, pl.ds(base + low, ROWS)] for t in range(SOME)]
                for g, k in uses(low):
                    total = mine[g][0] * window[0]
                    for t in range(1, SOME):
                        total += mine[g][t] * window[t]
                    at = i * BATCH + g
                    if first > 0:
                        total += img[at, k]
                    img[at, k] = total * scale[k] if first + SOME == steps else total
        for g in range(BATCH):
            for k in range(count, PAD):
                img[i * BATCH + g, k] = jnp.zeros((ROWS, width), F32)

    @pl.loop(1, 3)
    def _(i):
        correlate(i)

    order = (0, 2, 1, 3)
    for c in order:
        fill("z", c)
        reduce_step("z", 1, c)
    take_edges(rec_edges, rec32, 0)

    @pl.loop(0, 2)
    def _(i):
        correlate(i * 3)

    for c in order:
        fill("x", c)
        reduce_step("x", 1, c)
    for c in order:
        reduce_step("z", 2, c)
    take_edges(src_edges, src32, 1)
    for c in order:
        reduce_step("x", 2, c)
    for c in order:
        reduce_step("z", 3, c)
    for c in order:
        arrived["x", c].wait_recv()
    for half in range(2):
        for q in range(4):
            send_x[half * 4 + q] = encode(reduce_end("x", half, q))
    second_x = []
    for d in range(1, NUM_Z):
        other = wrap(z + d, NUM_Z)
        second_x.append(push(send_x.at[other], in_x.at[d - 1], at_z(other)))
    for c in order:
        reduce_step("z", 4, c)
    for c in order:
        arrived["z", c].wait_recv()
    for half in range(2):
        for q in range(2):
            send_z[half * 2 + q] = encode(reduce_end("z", half, q))
    second_z = []
    for d in range(1, NUM_X):
        other = wrap(x + d, NUM_X)
        second_z.append(push(send_z.at[other], in_z.at[d - 1], at_x(other)))

    total = decode(send_x[z])
    for d in range(1, NUM_Z):
        second_x[d - 1].wait_recv()
        total += decode(in_x[d - 1])
    pair_out[0] = encode(total)
    pair_x = push(pair_out.at[0], pair_in.at[0], pair)
    total = decode(send_z[x])
    for d in range(1, NUM_X):
        second_z[d - 1].wait_recv()
        total += decode(in_z[d - 1])
    pair_out[1] = encode(total)
    pair_z = push(pair_out.at[1], pair_in.at[1], pair)

    mine_x = out.at[group_x(x, z // 4), z % 4]
    pair_x.wait_recv()
    mine_x[...] = encode(decode(pair_out[0]) + decode(pair_in[0]))
    third_x = [push(mine_x, mine_x, at_z(wrap(z + d, NUM_Z))) for d in range(1, NUM_Z)]
    mine_z = out.at[group_z(z), x]
    pair_z.wait_recv()
    mine_z[...] = encode(decode(pair_out[1]) + decode(pair_in[1]))
    third_z = [push(mine_z, mine_z, at_x(wrap(x + d, NUM_X))) for d in range(1, NUM_X)]

    def part(name, owner, half):
        if name == "z":
            return out.at[group_z(owner), pl.ds(half * 2, 2)]
        return out.at[group_x(owner, half)]

    def gather_step(name, j, c):
        n, here, device, _, _ = plans[name]
        way, hops, half = ring_chains(n)[c]
        if j > hops + 1:
            return
        if j > 1:
            arrived[name, c].wait_recv()
        if j <= hops:
            held = part(name, wrap(here - way * (j - 1), n), half)
            arrived[name, c] = push(held, held, device(wrap(here + way, n)))

    def unpack(g, start, quarters):
        for q in quarters:
            values = decode(out[g, q])
            for i in range(QUARTER):
                if q * QUARTER + i < count:
                    pen[q * QUARTER + i, pl.ds(start, ROWS)] = values[i]

    def update_source(i):
        base = pl.multiple_of(i * BATCH * ROWS, ROWS)
        for g in range(BATCH):
            unpack(i * BATCH + g, base + g * ROWS + rim, range(4))
        masks = [inside(base + g * ROWS, ROWS) for g in range(BATCH)]
        for first in range(0, steps, SOME):
            total = {}
            for low in range(spread):
                window = [rec32[first + t, pl.ds(base + low, ROWS)] for t in range(SOME)]
                for g, k in uses(low):
                    p = pen[k, pl.ds(base + g * ROWS + rim, ROWS)]
                    for t in range(SOME):
                        term = p * window[t]
                        total[g, t] = term if k == 0 else total[g, t] + term
            for g in range(BATCH):
                for t in range(SOME):
                    held[first + t, pl.ds(base + g * ROWS, ROWS)] = jnp.where(masks[g], total[g, t], 0.0)

    def update_receiver(i):
        base = pl.multiple_of(i * BATCH * ROWS, ROWS)
        for first in range(0, steps, SOME):
            total = {}
            for low in range(spread):
                window = [src32[first + t, pl.ds(base + low, ROWS)] for t in range(SOME)]
                for g, back in uses(low):
                    k = count - 1 - back
                    p = pen[k, pl.ds(base + low, ROWS)]
                    for t in range(SOME):
                        term = p * window[t]
                        total[g, t] = term if back == 0 else total[g, t] + term
            for g in range(BATCH):
                for t in range(SOME):
                    held[first + t, pl.ds(base + g * ROWS, ROWS)] = total[g, t]

    for copy in third_z:
        copy.wait_recv()
    for c in order:
        gather_step("z", 1, c)
    for copy in third_x:
        copy.wait_recv()
    for c in order:
        gather_step("x", 1, c)
    for c in order:
        gather_step("z", 2, c)
    for c in order:
        gather_step("x", 2, c)
    for c in order:
        gather_step("z", 3, c)
    for c in order:
        gather_step("x", 3, c)

    to_right = push(
        out.at[pl.ds(groups - edge, edge), pl.ds(1, 3)],
        out.at[pl.ds(groups, edge), pl.ds(1, 3)],
        right,
    )
    to_left = push(out.at[pl.ds(0, edge), pl.ds(0, 2)], out.at[pl.ds(groups + edge, edge), pl.ds(0, 2)], left)
    for c in order:
        gather_step("z", 4, c)

    @pl.loop(0, 2)
    def _(i):
        update_source(i * 3)

    for c in order:
        gather_step("z", 5, c)

    @pl.loop(1, 3)
    def _(i):
        update_source(i)

    unit_pair = unit_matrix(width, 2 * width)
    for t in range(steps):
        src_upd[t] = turned_pair(unit_pair, held[t]).reshape(src_upd.shape[1:])
    to_right.wait_recv()
    to_left.wait_recv()
    for g in range(edge):
        unpack(groups + g, g * ROWS, range(1, 4))
        unpack(groups + edge + g, rim + width + g * ROWS, range(2))

    @pl.loop(0, groups // BATCH)
    def _(i):
        update_receiver(i)

    for t in range(steps):
        rec_upd[t] = turned_pair(unit_pair, held[t]).reshape(rec_upd.shape[1:])
    for copy in started:
        copy.wait_send()


def local(strips, shots, source_field, receiver_field, shot_pos, offset_weight):
    src, rec = source_field[0], receiver_field[0]
    steps, _, _, width = src.shape
    rim = offset_weight.shape[0] // 2
    span, groups = width + 2 * rim, width // ROWS
    piece = (WORDS, ROWS, width)

    def words(*lead):
        return pltpu.VMEM(lead + piece, jnp.int32)

    wide = pltpu.VMEM((steps, span, width), F32)
    edges = pltpu.VMEM((2, 2, steps, rim, width), jnp.bfloat16)
    upd = jax.ShapeDtypeStruct(src.shape, F32)
    src_upd, rec_upd = pl.pallas_call(
        functools.partial(fused_kernel, strips, float(shots * steps)),
        out_shape=(upd, upd),
        in_specs=[SMEM, SMEM, VMEM, VMEM],
        out_specs=(VMEM, VMEM),
        scratch_shapes=[
            wide,
            wide,
            edges,
            edges,
            pltpu.VMEM((groups, PAD, ROWS, width), F32),
            words(groups + 2 * rim // ROWS, 4),
            pltpu.VMEM((offset_weight.shape[0], span, width), F32),
            pltpu.VMEM((steps, width, width), F32),
            words(4, 2),
            words(4, 4),
            words(2 * NUM_Z - 2, 2),
            words(2 * NUM_X - 2, 4),
            words(4),
            words(8),
            words(NUM_X - 1),
            words(NUM_Z - 1),
            words(2),
            words(2),
            pltpu.SemaphoreType.DMA((80,)),
            pltpu.SemaphoreType.DMA((80,)),
        ],
        compiler_params=pltpu.CompilerParams(
            collective_id=0, has_side_effects=True, vmem_limit_bytes=60 * 2**20
        ),
        name="fused",
    )(shot_pos, offset_weight, rec, src)
    return src_upd[None], rec_upd[None]


def solution(mesh):
    return jax.shard_map(
        functools.partial(local, mesh.shape["strip"], mesh.shape["shot"]),
        mesh=mesh,
        in_specs=(
            P("shot", None, None, None, "strip"),
            P("shot", None, None, None, "strip"),
            P("shot"),
            P(),
        ),
        out_specs=(P("shot", None, None, None, "strip"), P("shot", None, None, None, "strip")),
        check_vma=False,
    )
```

time: 748 us -> 70.9 us (0.09)
  the two profiles are of different devices: /device:TPU:40 before, /device:TPU:4 now
where the time goes in v2:
time: 70.9 us; the launch traced here: 70.7 us
  Pallas kernels  66 us (93%)
  local copies, waits for them, and re-layouts  3.36 us (5%)
  between operations  1.29 us (2%)
    pallas_call x1, Pallas kernels, local(): pl.pallas_call(functools.partial(fused_kernel, strips, float(shots * step...  66 us
    unnamed x4, local copies, waits for them, and re-layouts  3.36 us

profile of v2, /device:TPU:4, one launch (start us, length us, event | category | flops | bytes accessed | tf_op | source)
XLA Modules:
  0.0 70.7 jit_solution(6424732496240085295)
XLA Ops:
  1.3 66.0 %fused.1 = (f32[16,8,16,128]{3,2,1,0:T(8,128)}, f32[16,8,16,128]{3,2,1,0:T(8,128)}) custom-call(s32[1]{0:T(128)S(6)} %copy.8.shots_pos, s32[33]{0:T(128)} %weight.1, bf16[16,8,16,128]{3,2,1,0:T(8,128)(2,1)} %bitcast.6, bf16[16,8,16,128]{3,2,1,0:T(8,128)(2,1)} %bitcast.7), custom_call_target="tpu_custom_call" | custom-call | tf_op jit(solution)/shard_map/fused/pallas_call | solution.py:437
  67.3 0.0 copy-start
  67.3 2.4 %copy.9 = f32[1,16,8,16,128]{4,3,2,1,0:T(8,128)} copy(f32[1,16,8,16,128]{4,3,2,1,0:T(8,128)} %bitcast.5) | data formatting | bytes 2097152
  69.7 0.0 copy-done
  69.7 1.0 %copy.10 = f32[1,16,8,16,128]{4,3,2,1,0:T(8,128)} copy(f32[1,16,8,16,128]{4,3,2,1,0:T(8,128)S(1)} %bitcast.4) | data formatting | bytes 2097152
Async XLA Ops:
  67.3 2.4 %copy-start = (f32[16,8,16,128]{3,2,1,0:T(8,128)S(1)}, f32[16,8,16,128]{3,2,1,0:T(8,128)}, u32[]{:S(2)}) copy-start(f32[16,8,16,128]{3,2,1,0:T(8,128)} %get-tuple-element.5) | copy-start | bytes 3145732

commit v3 on v2

v3 whole, which is shorter than its diff:
```python
import functools

import jax
import jax.numpy as jnp
from jax import lax
from jax.experimental import pallas as pl
from jax.experimental.pallas import tpu as pltpu
from jax.sharding import PartitionSpec as P

MESH = pl.DeviceIdType.MESH
VMEM = pl.BlockSpec(memory_space=pltpu.VMEM)
SMEM = pl.BlockSpec(memory_space=pltpu.SMEM)
HBM = pl.BlockSpec(memory_space=pltpu.HBM)
F32 = jnp.float32

NUM_X, NUM_Z, NUM_Y = 4, 8, 2
ROWS = 8
BATCH, SOME = 4, 8
PAD = 36
QUARTER = PAD // 4
WORDS = (QUARTER + 1) // 2
TINY, LIMIT, STEPS_2 = 1e-30, 32767.0, 16.0


def unit_matrix(rows, columns):
    i = lax.broadcasted_iota(jnp.int32, (rows, columns), 0)
    j = lax.broadcasted_iota(jnp.int32, (rows, columns), 1)
    return jnp.where(lax.rem(j, rows) == i, 1.0, 0.0).astype(jnp.bfloat16)


def turned(unit, values):
    return lax.dot_general(unit, values, (((1,), (1,)), ((), ())), preferred_element_type=F32)


def turned_pair(unit, values):
    high = values.astype(jnp.bfloat16)
    low = (values - high.astype(F32)).astype(jnp.bfloat16)
    return turned(unit, jnp.concatenate([high, low], axis=1))


def encode(values):
    top = jnp.maximum(jnp.max(jnp.abs(values), axis=0), TINY)
    code = jnp.ceil(jnp.log2(top) * STEPS_2)
    scaled = jnp.round(values * (LIMIT / jnp.exp2(code * (1.0 / STEPS_2))))
    whole = jnp.clip(scaled, -LIMIT, LIMIT).astype(jnp.int32)
    low = jnp.concatenate([whole[WORDS:], code.astype(jnp.int32)[None]])
    return (whole[:WORDS] << 16) | (low & 0xFFFF)


def decode(words):
    high, low = words >> 16, (words << 16) >> 16
    scale = jnp.exp2(low[WORDS - 1].astype(F32) * (1.0 / STEPS_2)) * (1.0 / LIMIT)
    return jnp.concatenate([high, low[: WORDS - 1]]).astype(F32) * scale


def ring_chains(n):
    far, near = n // 2, n // 2 - 1
    ways = [(1, 0), (-1, 2), (1, 1), (-1, 3)]
    return [(way, far, q) for way, q in ways] + [(-way, near, q) for way, q in ways]


def fused_kernel(
    strips,
    terms_count,
    shots_pos,
    rec_hbm,
    src_hbm,
    weight_hbm,
    src_upd,
    rec_upd,
    rec,
    src,
    weight,
    local,
    rec32,
    src32,
    edge_out,
    edge_in,
    img,
    out,
    pen,
    stage_z,
    stage_x,
    slot_z,
    slot_x,
    send_z,
    send_x,
    in_z,
    in_x,
    rim_in,
    send,
    recv,
    plane_send,
    plane_recv,
    rim_send,
    rim_recv,
):
    steps, width = rec.shape[0], rec.shape[-1]
    count = weight.shape[0]
    rim = count // 2
    edge = rim // ROWS
    groups = width // ROWS
    shot, strip = lax.axis_index("shot"), lax.axis_index("strip")
    x, z, y = shot // (NUM_Z * NUM_Y), shot // NUM_Y % NUM_Z, shot % NUM_Y

    def at_x(i):
        return {"shot": (i * NUM_Z + z) * NUM_Y + y}

    def at_z(i):
        return {"shot": (x * NUM_Z + i) * NUM_Y + y}

    def wrap(i, n):
        return lax.rem(i + n, n)

    def at_xy(i, j):
        return {"shot": (i * NUM_Z + z) * NUM_Y + j}

    left, right = {"strip": wrap(strip - 1, strips)}, {"strip": wrap(strip + 1, strips)}
    plane, sources = [], []
    for dx in (2, 1, 3, 0):
        for dy in (1, 0):
            if dx or dy:
                plane.append((wrap(x + dx, NUM_X), y + dy - 2 * dy * y))
                sources.append((wrap(x - dx, NUM_X), y + dy - 2 * dy * y))
    line = [wrap(z + d, NUM_Z) for d in (4, 3, 5, 2, 6, 1, 7)]
    others = [at_xy(*place) for place in plane] + [at_z(i) for i in line] + [left, right]
    barrier = pltpu.get_barrier_semaphore()
    loads = []
    for i, (there, here) in enumerate(((rec_hbm, rec), (src_hbm, src), (weight_hbm, weight))):
        loads.append(pltpu.make_async_copy(there, here, local.at[i]))
        loads[-1].start()
    for other in others:
        pl.semaphore_signal(barrier, inc=1, device_id=other, device_id_type=MESH)

    def group_z(i):
        return NUM_Z // 2 + i

    def group_xy(i, j):
        return NUM_Y * i + j + i // (NUM_X // 2) * NUM_Z

    def terms(group, q):
        return img[group, q * QUARTER : (q + 1) * QUARTER]

    started = []

    def push(src_ref, dst_ref, device):
        i = len(started)
        copy = pltpu.make_async_remote_copy(
            src_ref=src_ref,
            dst_ref=dst_ref,
            send_sem=send.at[i],
            recv_sem=recv.at[i],
            device_id=device,
            device_id_type=MESH,
        )
        copy.start()
        started.append(copy)
        return copy

    chains = ring_chains(NUM_Z)
    firsts = [sum(hops for _, hops, _ in chains[:c]) for c in range(len(chains))]
    arrived = [None] * len(chains)

    def reduce_step(j):
        for c, (way, hops, q) in enumerate(chains):
            if j > hops:
                continue
            group = group_z(wrap(z + way * (hops + 1 - j), NUM_Z))
            if j == 1:
                held_here = stage_z.at[c]
                held_here[...] = encode(terms(group, q))
            else:
                held_here = slot_z.at[firsts[c] + j - 2]
                arrived[c].wait_recv()
                held_here[...] = encode(decode(held_here[...]) + terms(group, q))
            arrived[c] = push(held_here, slot_z.at[firsts[c] + j - 1], at_z(wrap(z + way, NUM_Z)))

    def gather_step(j):
        for c, (way, hops, q) in enumerate(chains):
            if j > hops + 1:
                continue
            if j > 1:
                arrived[c].wait_recv()
            if j <= hops:
                piece = out.at[group_z(wrap(z - way * (j - 1), NUM_Z)), q]
                arrived[c] = push(piece, piece, at_z(wrap(z + way, NUM_Z)))

    unit = unit_matrix(width, width)
    pos = shots_pos[0]

    def inside(first, rows):
        cells = strip * width + first + lax.broadcasted_iota(jnp.int32, (rows, width), 0)
        return jnp.abs(cells - pos) <= width * strips // 4

    def take_in(field, wide, which, mask):
        for t in range(steps):
            value = turned(unit, field[t].reshape(width, width))
            if mask is not None:
                value = jnp.where(mask, value, 0.0)
            wide[t, rim : rim + width] = value
            edge_out[which, 0, t] = value[width - rim :].astype(jnp.bfloat16)
            edge_out[which, 1, t] = value[:rim].astype(jnp.bfloat16)

    def push_edges(which):
        return [push(edge_out.at[which, side], edge_in.at[which, side], (right, left)[side]) for side in range(2)]

    def take_edges(copies, wide, which):
        for copy in copies:
            copy.wait_recv()
        has_left = jnp.full((rim, width), strip, jnp.int32) > 0
        has_right = jnp.full((rim, width), strip, jnp.int32) < strips - 1
        for t in range(steps):
            wide[t, 0:rim] = jnp.where(has_left, edge_in[which, 0, t].astype(F32), 0.0)
            wide[t, rim + width : 2 * rim + width] = jnp.where(has_right, edge_in[which, 1, t].astype(F32), 0.0)

    loads[0].wait()
    take_in(rec, rec32, 0, None)
    pl.semaphore_wait(barrier, len(others))
    rec_edges = push_edges(0)
    loads[1].wait()
    take_in(src, src32, 1, inside(0, width))
    src_edges = push_edges(1)

    loads[2].wait()
    scale = [weight[k].astype(F32) * (1.0 / terms_count) for k in range(count)]

    def uses(low, batch):
        return [(g, low - g * ROWS) for g in range(batch) if 0 <= low - g * ROWS < count]

    def correlate(start, batch):
        base = pl.multiple_of(start * ROWS, ROWS)
        for first in range(0, steps, SOME):
            mine = [
                [src32[first + t, pl.ds(base + g * ROWS + rim, ROWS)] for t in range(SOME)] for g in range(batch)
            ]
            for low in range(count + (batch - 1) * ROWS):
                window = [rec32[first + t, pl.ds(base + low, ROWS)] for t in range(SOME)]
                for g, k in uses(low, batch):
                    total = mine[g][0] * window[0]
                    for t in range(1, SOME):
                        total += mine[g][t] * window[t]
                    if first > 0:
                        total += img[start + g, k]
                    img[start + g, k] = total * scale[k] if first + SOME == steps else total
        for g in range(batch):
            for k in range(count, PAD):
                img[start + g, k] = jnp.zeros((ROWS, width), F32)

    @pl.loop(1, groups // BATCH - 1)
    def _(i):
        correlate(i * BATCH, BATCH)

    reduce_step(1)

    @pl.loop(0, 2)
    def _(i):
        correlate(edge + i * (groups - 3 * edge), edge)

    def place_of(i, far):
        column = lax.rem(x + i // NUM_Y, 2)
        return (3 * column if far else 1 + column), lax.rem(y + i + 1, NUM_Y)

    def order_of(i, j):
        return i * NUM_Y + j

    my_order = order_of(x, y)

    def plane_copy(place):
        return pltpu.make_async_remote_copy(
            src_ref=stage_x.at[order_of(*place)],
            dst_ref=slot_x.at[my_order],
            send_sem=plane_send.at[order_of(*place)],
            recv_sem=plane_recv.at[my_order],
            device_id=at_xy(*place),
            device_id_type=MESH,
        )

    def push_plane(place):
        for q in range(4):
            stage_x[order_of(*place), q] = encode(terms(group_xy(*place), q))

        @pl.when(order_of(*place) != my_order)
        def _():
            plane_copy(place).start()

    every = [(i, j) for i in range(NUM_X) for j in range(NUM_Y)]
    for i in range(NUM_X):
        push_plane(place_of(i, False))
    reduce_step(2)
    take_edges(rec_edges, rec32, 0)

    @pl.loop(0, 2)
    def _(i):
        correlate(i * (groups - edge), edge)

    for i in range(NUM_X):
        push_plane(place_of(i, True))
    reduce_step(3)
    reduce_step(4)

    for q in range(4):
        slot_x[my_order, q] = stage_x[my_order, q]
    for i, place in enumerate(every):

        @pl.when(i != my_order)
        def _():
            pltpu.make_async_remote_copy(
                src_ref=stage_x.at[i],
                dst_ref=slot_x.at[i],
                send_sem=plane_send.at[i],
                recv_sem=plane_recv.at[i],
                device_id=at_xy(*place),
                device_id_type=MESH,
            ).wait()

    for q in range(4):
        total = decode(slot_x[0, q])
        for i in range(1, len(every)):
            total += decode(slot_x[i, q])
        send_x[q] = encode(total)
    second_xy = [push(send_x.at[i % 4], in_x.at[j], at_z(i)) for j, i in enumerate(line)]

    for q in range(4):
        total = terms(group_z(z), q)
        for c, (_, hops, own) in enumerate(chains):
            if own == q:
                arrived[c].wait_recv()
                total += decode(slot_z[firsts[c] + hops - 1])
        send_z[q] = encode(total)
    second_z = [push(send_z.at[i], in_z.at[n], at_xy(i, j)) for n, (i, j) in enumerate(plane)]

    total = decode(send_x[z % 4])
    for j in range(len(line)):
        second_xy[j].wait_recv()
        total += decode(in_x[j])
    mine_xy = out.at[group_xy(x, y), z % 4]
    mine_xy[...] = encode(total)
    third_xy = [push(mine_xy, mine_xy, at_z(wrap(z + d, NUM_Z))) for d in (2, 1, NUM_Z - 1)]
    total = decode(send_z[x])
    for j in range(len(plane)):
        second_z[j].wait_recv()
        total += decode(in_z[j])
    mine_z = out.at[group_z(z), x]
    mine_z[...] = encode(total)
    third_z = [push(mine_z, mine_z, at_x(wrap(x + d, NUM_X))) for d in (2, 1, 3)]

    def unpack(g, start, quarters):
        for q in quarters:
            values = decode(out[g, q])
            for i in range(QUARTER):
                if q * QUARTER + i < count:
                    pen[q * QUARTER + i, pl.ds(start, ROWS)] = values[i]

    def update_source(places):
        @pl.loop(0, len(places))
        def _(i):
            g = places[0]
            for j in range(1, len(places)):
                g = jnp.where(i == j, places[j], g)
            base = pl.multiple_of(g * ROWS, ROWS)
            unpack(g, base + rim, range(4))
            mask = inside(base, ROWS)
            total = [None] * steps
            for k in range(count):
                p = pen[k, pl.ds(base + rim, ROWS)]
                for t in range(steps):
                    term = p * rec32[t, pl.ds(base + k, ROWS)]
                    total[t] = term if k == 0 else total[t] + term
            for t in range(steps):
                src_upd[t, pl.ds(base, ROWS)] = jnp.where(mask, total[t], 0.0)

    def update_receiver(i):
        base = pl.multiple_of(i * BATCH * ROWS, ROWS)
        for first in range(0, steps, SOME):
            total = {}
            for low in range(count + (BATCH - 1) * ROWS):
                window = [src32[first + t, pl.ds(base + low, ROWS)] for t in range(SOME)]
                for g, back in uses(low, BATCH):
                    k = count - 1 - back
                    p = pen[k, pl.ds(base + low, ROWS)]
                    for t in range(SOME):
                        term = p * window[t]
                        total[g, t] = term if back == 0 else total[g, t] + term
            for g in range(BATCH):
                for t in range(SOME):
                    rec_upd[first + t, pl.ds(base + g * ROWS, ROWS)] = total[g, t]

    for copy in third_xy:
        copy.wait_recv()
    whole = out.at[group_xy(x, y)]
    high = x // (NUM_X // 2)
    rim_out = push(
        out.at[group_xy(x, y), pl.ds(high, 3)],
        rim_in,
        {"shot": shot, "strip": wrap(strip - 1 + 2 * high, strips)},
    )
    rim_places = [(i, j) for i in (0, NUM_X - 1) for j in range(NUM_Y)]

    def rim_slot(i, j):
        return groups + i // (NUM_X // 2) * NUM_Y + j

    def rim_copy(place, to, i):
        piece = out.at[rim_slot(*place), pl.ds(place[0] // (NUM_X // 2), 3)]
        return pltpu.make_async_remote_copy(
            src_ref=piece,
            dst_ref=piece,
            send_sem=rim_send.at[i],
            recv_sem=rim_recv.at[order_of(*place)],
            device_id=at_xy(*to),
            device_id_type=MESH,
        )

    def pass_rims():
        rim_out.wait_recv()
        for place in rim_places:

            @pl.when(order_of(*place) == my_order)
            def _():
                for q in range(3):
                    out[rim_slot(*place), place[0] // (NUM_X // 2) + q] = rim_in[q]
                for i, to in enumerate(every):
                    if to != place:
                        rim_copy(place, to, i).start()

    def wait_rims():
        for place in rim_places:

            @pl.when(order_of(*place) == my_order)
            def _():
                for i, to in enumerate(every):
                    if to != place:
                        rim_copy(place, to, i).wait_send()

            @pl.when(order_of(*place) != my_order)
            def _():
                rim_copy(place, place, 0).wait_recv()

    fourth_xy = [push(whole, whole, at_xy(*place)) for place in plane]
    for copy in third_z:
        copy.wait_recv()

    def along(d):
        return group_z(wrap(z + d, NUM_Z))

    def over_plane(first, last):
        for copy in fourth_xy[first:last]:
            copy.wait_recv()
        return [group_xy(*place) for place in sources[first:last]]

    gather_step(1)
    take_edges(src_edges, src32, 1)
    update_source([along(0), group_xy(x, y)])
    gather_step(2)
    update_source([along(1), along(-1)])
    gather_step(3)
    pass_rims()
    update_source([along(2), along(-2)])
    gather_step(4)
    update_source([along(3), along(-3)])
    update_source(over_plane(0, 3))
    gather_step(5)
    update_source(over_plane(3, 7) + [along(4)])

    @pl.loop(1, 3)
    def _(i):
        update_receiver(i)

    wait_rims()
    for g in range(edge):
        unpack(groups + edge + g, g * ROWS, range(1, 4))
        unpack(groups + g, rim + width + g * ROWS, range(2))

    @pl.loop(0, 2)
    def _(i):
        update_receiver(i * 3)

    for copy in started:
        copy.wait_send()


def finish_kernel(src_rows, rec_rows, src_upd, rec_upd, turned_src, turned_rec, done):
    steps, width = src_rows.shape[:2]
    unit_pair = unit_matrix(width, 2 * width)
    copies = []
    for t in range(steps):
        for i, (rows, held, whole) in enumerate(
            ((src_rows, turned_src, src_upd), (rec_rows, turned_rec, rec_upd))
        ):
            held[t] = turned_pair(unit_pair, rows[t]).reshape(held.shape[1:])
            copy = pltpu.make_async_copy(held.at[t], whole.at[t], done.at[i, t])
            copy.start()
            copies.append(copy)
    for copy in copies:
        copy.wait()


def local(strips, shots, source_field, receiver_field, shot_pos, offset_weight):
    src, rec = source_field[0], receiver_field[0]
    steps, _, _, width = src.shape
    rim = offset_weight.shape[0] // 2
    span, groups = width + 2 * rim, width // ROWS
    piece = (WORDS, ROWS, width)

    def words(*lead):
        return pltpu.VMEM(lead + piece, jnp.int32)

    wide = pltpu.VMEM((steps, span, width), F32)
    edges = pltpu.VMEM((2, 2, steps, rim, width), jnp.bfloat16)
    rows = jax.ShapeDtypeStruct((steps, width, width), F32)
    src_rows, rec_rows = pl.pallas_call(
        functools.partial(fused_kernel, strips, float(shots * steps)),
        out_shape=(rows, rows),
        in_specs=[SMEM, HBM, HBM, HBM],
        out_specs=(VMEM, VMEM),
        scratch_shapes=[
            pltpu.VMEM(rec.shape, rec.dtype),
            pltpu.VMEM(src.shape, src.dtype),
            pltpu.SMEM(offset_weight.shape, offset_weight.dtype),
            pltpu.SemaphoreType.DMA((3,)),
            wide,
            wide,
            edges,
            edges,
            pltpu.VMEM((groups, PAD, ROWS, width), F32),
            words(groups + 2 * rim // ROWS, 4),
            pltpu.VMEM((offset_weight.shape[0], span, width), F32),
            words(8),
            words(NUM_X * NUM_Y, 4),
            words(4 * NUM_Z - 4),
            words(NUM_X * NUM_Y, 4),
            words(4),
            words(4),
            words(7),
            words(7),
            words(3),
            pltpu.SemaphoreType.DMA((96,)),
            pltpu.SemaphoreType.DMA((96,)),
            pltpu.SemaphoreType.DMA((NUM_X * NUM_Y,)),
            pltpu.SemaphoreType.DMA((NUM_X * NUM_Y,)),
            pltpu.SemaphoreType.DMA((NUM_X * NUM_Y,)),
            pltpu.SemaphoreType.DMA((NUM_X * NUM_Y,)),
        ],
        compiler_params=pltpu.CompilerParams(
            collective_id=0, has_side_effects=True, vmem_limit_bytes=28 * 2**20
        ),
        name="fused",
    )(shot_pos, rec, src, offset_weight)

    upd = jax.ShapeDtypeStruct(src.shape, F32)
    src_upd, rec_upd = pl.pallas_call(
        finish_kernel,
        out_shape=(upd, upd),
        in_specs=[VMEM, VMEM],
        out_specs=(HBM, HBM),
        scratch_shapes=[
            pltpu.VMEM(src.shape, F32),
            pltpu.VMEM(src.shape, F32),
            pltpu.SemaphoreType.DMA((2, steps)),
        ],
        compiler_params=pltpu.CompilerParams(vmem_limit_bytes=28 * 2**20),
        name="finish",
    )(src_rows, rec_rows)
    return src_upd[None], rec_upd[None]


def solution(mesh):
    return jax.shard_map(
        functools.partial(local, mesh.shape["strip"], mesh.shape["shot"]),
        mesh=mesh,
        in_specs=(
            P("shot", None, None, None, "strip"),
            P("shot", None, None, None, "strip"),
            P("shot"),
            P(),
        ),
        out_specs=(P("shot", None, None, None, "strip"), P("shot", None, None, None, "strip")),
        check_vma=False,
    )
```

time: 70.9 us -> 65.1 us (0.918)
  the two profiles are of different devices: /device:TPU:4 before, /device:TPU:16 now
where the time goes in v3:
time: 65.1 us; the launch traced here: 64.9 us
  Pallas kernels  60.9 us (94%)
  local copies, waits for them, and re-layouts  2.73 us (4%)
  between operations  1.29 us (2%)
    pallas_call x1, Pallas kernels, local(): pl.pallas_call(functools.partial(fused_kernel, strips, float(shots * step...  59.1 us
    unnamed x6, local copies, waits for them, and re-layouts  2.73 us
    pallas_call x1, Pallas kernels, local(): pl.pallas_call(finish_kernel, out_shape=(upd, upd), in_specs=[VMEM, VMEM]...  1.77 us

profile of v3, /device:TPU:16, one launch (start us, length us, event | category | flops | bytes accessed | tf_op | source)
XLA Modules:
  0.0 64.9 jit_solution(8385327230052656052)
XLA Ops:
  1.3 0.0 copy-start.2
  1.3 0.6 copy-done.2
  1.9 0.0 copy-start
  1.9 1.0 %copy-done = bf16[1,16,8,16,128]{4,3,2,1,0:T(8,128)(2,1)S(1)} copy-done((bf16[1,16,8,16,128]{4,3,2,1,0:T(8,128)(2,1)S(1)}, bf16[1,16,8,16,128]{4,3,2,1,0:T(8,128)(2,1)}, u32[]{:S(2)}) %copy-start) | copy-done | bytes 524312
  3.0 0.0 copy-start.1
  3.0 1.0 %copy-done.1 = bf16[1,16,8,16,128]{4,3,2,1,0:T(8,128)(2,1)S(1)} copy-done((bf16[1,16,8,16,128]{4,3,2,1,0:T(8,128)(2,1)S(1)}, bf16[1,16,8,16,128]{4,3,2,1,0:T(8,128)(2,1)}, u32[]{:S(2)}) %copy-start.1) | copy-done | bytes 524312
  4.0 59.1 %fused.1 = (f32[16,128,128]{2,1,0:T(8,128)S(1)}, f32[16,128,128]{2,1,0:T(8,128)S(1)}) custom-call(s32[1]{0:T(128)S(6)} %copy.6.shots_pos, bf16[16,8,16,128]{3,2,1,0:T(8,128)(2,1)S(1)} %bitcast.4, bf16[16,8,16,128]{3,2,1,0:T(8,128)(2,1)S(1)} %bitcast.5, s32[33]{0:T(128)S(1)} %copy-done.2), custom_call_target="tpu_custom_call" | custom-call | tf_op jit(solution)/shard_map/fused/pallas_call | solution.py:510
  63.1 1.8 %finish.1 = (f32[16,8,16,128]{3,2,1,0:T(8,128)}, f32[16,8,16,128]{3,2,1,0:T(8,128)}) custom-call(f32[16,128,128]{2,1,0:T(8,128)S(1)} %get-tuple-element.6.src_rows, f32[16,128,128]{2,1,0:T(8,128)S(1)} %get-tuple-element.7.rec_rows), custom_call_target="tpu_custom_call" | custom-call | tf_op jit(solution)/shard_map/finish/pallas_call | solution.py:550
Async XLA Ops:
  1.3 0.7 %copy-start.2 = (s32[33]{0:T(128)S(1)}, s32[33]{0:T(128)}, u32[]{:S(2)}) copy-start(s32[33]{0:T(128)} %weight_hbm.1) | copy-start | bytes 400
  1.9 1.0 %copy-start = (bf16[1,16,8,16,128]{4,3,2,1,0:T(8,128)(2,1)S(1)}, bf16[1,16,8,16,128]{4,3,2,1,0:T(8,128)(2,1)}, u32[]{:S(2)}) copy-start(bf16[1,16,8,16,128]{4,3,2,1,0:T(8,128)(2,1)} %param.5) | copy-start | bytes 1572868
  3.0 1.0 %copy-start.1 = (bf16[1,16,8,16,128]{4,3,2,1,0:T(8,128)(2,1)S(1)}, bf16[1,16,8,16,128]{4,3,2,1,0:T(8,128)(2,1)}, u32[]{:S(2)}) copy-start(bf16[1,16,8,16,128]{4,3,2,1,0:T(8,128)(2,1)} %param.4) | copy-start | bytes 1572868

commit v4 on v3

--- a/solution.py
+++ b/solution.py
@@ -38,6 +38,10 @@
     return turned(unit, jnp.concatenate([high, low], axis=1))
 
 
+def slot_of(k, rim):
+    return k if k <= rim else k + 1
+
+
 def encode(values):
     top = jnp.maximum(jnp.max(jnp.abs(values), axis=0), TINY)
     code = jnp.ceil(jnp.log2(top) * STEPS_2)
@@ -51,12 +55,6 @@
     high, low = words >> 16, (words << 16) >> 16
     scale = jnp.exp2(low[WORDS - 1].astype(F32) * (1.0 / STEPS_2)) * (1.0 / LIMIT)
     return jnp.concatenate([high, low[: WORDS - 1]]).astype(F32) * scale
-
-
-def ring_chains(n):
-    far, near = n // 2, n // 2 - 1
-    ways = [(1, 0), (-1, 2), (1, 1), (-1, 3)]
-    return [(way, far, q) for way, q in ways] + [(-way, near, q) for way, q in ways]
 
 
 def fused_kernel(
@@ -157,33 +155,52 @@
         started.append(copy)
         return copy
 
-    chains = ring_chains(NUM_Z)
-    firsts = [sum(hops for _, hops, _ in chains[:c]) for c in range(len(chains))]
-    arrived = [None] * len(chains)
-
-    def reduce_step(j):
-        for c, (way, hops, q) in enumerate(chains):
-            if j > hops:
-                continue
-            group = group_z(wrap(z + way * (hops + 1 - j), NUM_Z))
-            if j == 1:
-                held_here = stage_z.at[c]
-                held_here[...] = encode(terms(group, q))
-            else:
-                held_here = slot_z.at[firsts[c] + j - 2]
-                arrived[c].wait_recv()
-                held_here[...] = encode(decode(held_here[...]) + terms(group, q))
-            arrived[c] = push(held_here, slot_z.at[firsts[c] + j - 1], at_z(wrap(z + way, NUM_Z)))
-
-    def gather_step(j):
-        for c, (way, hops, q) in enumerate(chains):
-            if j > hops + 1:
-                continue
-            if j > 1:
-                arrived[c].wait_recv()
-            if j <= hops:
-                piece = out.at[group_z(wrap(z - way * (j - 1), NUM_Z)), q]
-                arrived[c] = push(piece, piece, at_z(wrap(z + way, NUM_Z)))
+    far = ((1, 0), (-1, 2), (1, 1), (-1, 3))
+    near = tuple((-way, q) for way, q in far)
+
+    def z_group(d):
+        return group_z(wrap(z + d, NUM_Z))
+
+    def send_z_step(held_here, to, message, c):
+        return push(held_here, slot_z.at[message * len(far) + c], at_z(wrap(z + to, NUM_Z)))
+
+    def start_far():
+        copies = []
+        for c, (way, q) in enumerate(far):
+            stage_z[c] = encode(terms(z_group(4 * way), q))
+            copies.append(send_z_step(stage_z.at[c], way, 0, c))
+        return copies
+
+    def start_near():
+        copies = []
+        for c, (way, q) in enumerate(near):
+            stage_z[4 + c] = encode(terms(z_group(3 * way), q))
+            copies.append(send_z_step(stage_z.at[4 + c], way, 4, c))
+        return copies
+
+    def go_on(ways, copies, d, message):
+        passed = []
+        for c, (way, q) in enumerate(ways):
+            held_here = slot_z.at[message[0] * len(far) + c]
+            copies[c].wait_recv()
+            total = decode(held_here[...]) + terms(z_group(d * way), q)
+            held_here[...] = encode(total)
+            passed.append(send_z_step(held_here, way, message[1], c))
+        return passed
+
+    def pass_quarters(ways, copies, d, steps_on):
+        passed = [[] for _ in steps_on]
+        for c, (way, q) in enumerate(ways):
+            if copies is not None:
+                copies[c].wait_recv()
+            piece = out.at[z_group(-d * way), q]
+            for made, to in zip(passed, steps_on):
+                made.append(push(piece, piece, at_z(wrap(z + to * way, NUM_Z))))
+        return passed
+
+    def land(copies):
+        for copy in copies:
+            copy.wait_recv()
 
     unit = unit_matrix(width, width)
     pos = shots_pos[0]
@@ -240,17 +257,17 @@
                     for t in range(1, SOME):
                         total += mine[g][t] * window[t]
                     if first > 0:
-                        total += img[start + g, k]
-                    img[start + g, k] = total * scale[k] if first + SOME == steps else total
+                        total += img[start + g, slot_of(k, rim)]
+                    img[start + g, slot_of(k, rim)] = total * scale[k] if first + SOME == steps else total
         for g in range(batch):
-            for k in range(count, PAD):
-                img[start + g, k] = jnp.zeros((ROWS, width), F32)
-
-    @pl.loop(1, groups // BATCH - 1)
-    def _(i):
-        correlate(i * BATCH, BATCH)
-
-    reduce_step(1)
+            for empty in set(range(PAD)) - {slot_of(k, rim) for k in range(count)}:
+                img[start + g, empty] = jnp.zeros((ROWS, width), F32)
+
+    nearer = z // (NUM_Z // 2)
+    correlate((2 - nearer) * BATCH, BATCH)
+    far_0 = start_far()
+    correlate((1 + nearer) * BATCH, BATCH)
+    near_0 = start_near()
 
     @pl.loop(0, 2)
     def _(i):
@@ -286,7 +303,8 @@
     every = [(i, j) for i in range(NUM_X) for j in range(NUM_Y)]
     for i in range(NUM_X):
         push_plane(place_of(i, False))
-    reduce_step(2)
+    far_1 = go_on(far, far_0, 3, (0, 1))
+    near_1 = go_on(near, near_0, 2, (4, 5))
     take_edges(rec_edges, rec32, 0)
 
     @pl.loop(0, 2)
@@ -295,8 +313,9 @@
 
     for i in range(NUM_X):
         push_plane(place_of(i, True))
-    reduce_step(3)
-    reduce_step(4)
+    far_2 = go_on(far, far_1, 2, (1, 2))
+    near_2 = go_on(near, near_1, 1, (5, 6))
+    far_3 = go_on(far, far_2, 1, (2, 3))
 
     for q in range(4):
         slot_x[my_order, q] = stage_x[my_order, q]
@@ -322,10 +341,11 @@
 
     for q in range(4):
         total = terms(group_z(z), q)
-        for c, (_, hops, own) in enumerate(chains):
-            if own == q:
-                arrived[c].wait_recv()
-                total += decode(slot_z[firsts[c] + hops - 1])
+        for ways, copies, message in ((far, far_3, 3), (near, near_2, 6)):
+            for c, (_, own) in enumerate(ways):
+                if own == q:
+                    copies[c].wait_recv()
+                    total += decode(slot_z[message * len(far) + c])
         send_z[q] = encode(total)
     second_z = [push(send_z.at[i], in_z.at[n], at_xy(i, j)) for n, (i, j) in enumerate(plane)]
 
@@ -347,9 +367,9 @@
     def unpack(g, start, quarters):
         for q in quarters:
             values = decode(out[g, q])
-            for i in range(QUARTER):
-                if q * QUARTER + i < count:
-                    pen[q * QUARTER + i, pl.ds(start, ROWS)] = values[i]
+            for k in range(count):
+                if slot_of(k, rim) // QUARTER == q:
+                    pen[k, pl.ds(start, ROWS)] = values[slot_of(k, rim) % QUARTER]
 
     def update_source(places):
         @pl.loop(0, len(places))
@@ -390,7 +410,7 @@
     whole = out.at[group_xy(x, y)]
     high = x // (NUM_X // 2)
     rim_out = push(
-        out.at[group_xy(x, y), pl.ds(high, 3)],
+        out.at[group_xy(x, y), pl.ds(2 * high, 2)],
         rim_in,
         {"shot": shot, "strip": wrap(strip - 1 + 2 * high, strips)},
     )
@@ -400,7 +420,7 @@
         return groups + i // (NUM_X // 2) * NUM_Y + j
 
     def rim_copy(place, to, i):
-        piece = out.at[rim_slot(*place), pl.ds(place[0] // (NUM_X // 2), 3)]
+        piece = out.at[rim_slot(*place), pl.ds(place[0] // (NUM_X // 2) * 2, 2)]
         return pltpu.make_async_remote_copy(
             src_ref=piece,
             dst_ref=piece,
@@ -416,8 +436,8 @@
 
             @pl.when(order_of(*place) == my_order)
             def _():
-                for q in range(3):
-                    out[rim_slot(*place), place[0] // (NUM_X // 2) + q] = rim_in[q]
+                for q in range(2):
+                    out[rim_slot(*place), place[0] // (NUM_X // 2) * 2 + q] = rim_in[q]
                 for i, to in enumerate(every):
                     if to != place:
                         rim_copy(place, to, i).start()
@@ -447,19 +467,23 @@
             copy.wait_recv()
         return [group_xy(*place) for place in sources[first:last]]
 
-    gather_step(1)
+    (far_0,) = pass_quarters(far, None, 0, (1,))
+    (near_0,) = pass_quarters(near, None, 0, (1,))
     take_edges(src_edges, src32, 1)
     update_source([along(0), group_xy(x, y)])
-    gather_step(2)
+    far_2, far_1 = pass_quarters(far, far_0, 1, (2, 1))
+    (near_1,) = pass_quarters(near, near_0, 1, (1,))
     update_source([along(1), along(-1)])
-    gather_step(3)
+    (near_2,) = pass_quarters(near, near_1, 2, (1,))
+    (far_3,) = pass_quarters(far, far_2, 3, (1,))
     pass_rims()
+    land(far_1)
     update_source([along(2), along(-2)])
-    gather_step(4)
+    land(near_2)
     update_source([along(3), along(-3)])
-    update_source(over_plane(0, 3))
-    gather_step(5)
-    update_source(over_plane(3, 7) + [along(4)])
+    land(far_3)
+    update_source([along(4)] + over_plane(0, 3))
+    update_source(over_plane(3, 7))
 
     @pl.loop(1, 3)
     def _(i):
@@ -467,7 +491,7 @@
 
     wait_rims()
     for g in range(edge):
-        unpack(groups + edge + g, g * ROWS, range(1, 4))
+        unpack(groups + edge + g, g * ROWS, range(2, 4))
         unpack(groups + g, rim + width + g * ROWS, range(2))
 
     @pl.loop(0, 2)
@@ -506,7 +530,7 @@
 
     wide = pltpu.VMEM((steps, span, width), F32)
     edges = pltpu.VMEM((2, 2, steps, rim, width), jnp.bfloat16)
-    rows = jax.ShapeDtypeStruct((steps, width, width), F32)
+    rows = pltpu.VMEM((steps, width, width), F32)
     src_rows, rec_rows = pl.pallas_call(
         functools.partial(fused_kernel, strips, float(shots * steps)),
         out_shape=(rows, rows),
@@ -532,7 +556,7 @@
             words(4),
             words(7),
             words(7),
-            words(3),
+            words(2),
             pltpu.SemaphoreType.DMA((96,)),
             pltpu.SemaphoreType.DMA((96,)),
             pltpu.SemaphoreType.DMA((NUM_X * NUM_Y,)),
@@ -541,7 +565,7 @@
             pltpu.SemaphoreType.DMA((NUM_X * NUM_Y,)),
         ],
         compiler_params=pltpu.CompilerParams(
-            collective_id=0, has_side_effects=True, vmem_limit_bytes=28 * 2**20
+            collective_id=0, has_side_effects=True, vmem_limit_bytes=56 * 2**20
         ),
         name="fused",
     )(shot_pos, rec, src, offset_weight)

time: 65.1 us -> 62.3 us (0.957)
  local copies, waits for them, and re-layouts: 2.73 us -> 0 us
    unnamed x6 -> x0, local copies, waits for them, and re-layouts: 2.73 us -> none
where the time goes in v4:
time: 62.3 us; the launch traced here: 62.1 us
  Pallas kernels  60.9 us (98%)
  between operations  1.28 us (2%)
    pallas_call x1, Pallas kernels, local(): pl.pallas_call(functools.partial(fused_kernel, strips, float(shots * step...  59.1 us
    pallas_call x1, Pallas kernels, local(): pl.pallas_call(finish_kernel, out_shape=(upd, upd), in_specs=[VMEM, VMEM]...  1.78 us

profile of v4, /device:TPU:16, one launch (start us, length us, event | category | flops | bytes accessed | tf_op | source)
XLA Modules:
  0.0 62.1 jit_solution(6177216065036338143)
XLA Ops:
  1.3 59.1 %fused.1 = (f32[16,128,128]{2,1,0:T(8,128)S(1)}, f32[16,128,128]{2,1,0:T(8,128)S(1)}) custom-call(s32[1]{0:T(128)S(6)} %copy.6.shots_pos, bf16[16,8,16,128]{3,2,1,0:T(8,128)(2,1)} %bitcast.4, bf16[16,8,16,128]{3,2,1,0:T(8,128)(2,1)} %bitcast.5, s32[33]{0:T(128)} %weight_hbm.1), custom_call_target="tpu_custom_call" | custom-call | tf_op jit(solution)/shard_map/fused/pallas_call | solution.py:534
  60.4 1.8 %finish.1 = (f32[16,8,16,128]{3,2,1,0:T(8,128)}, f32[16,8,16,128]{3,2,1,0:T(8,128)}) custom-call(f32[16,128,128]{2,1,0:T(8,128)S(1)} %get-tuple-element.6.src_rows, f32[16,128,128]{2,1,0:T(8,128)S(1)} %get-tuple-element.7.rec_rows), custom_call_target="tpu_custom_call" | custom-call | tf_op jit(solution)/shard_map/finish/pallas_call | solution.py:574

commit v5 on v4

--- a/solution.py
+++ b/solution.py
@@ -474,9 +474,9 @@
     far_2, far_1 = pass_quarters(far, far_0, 1, (2, 1))
     (near_1,) = pass_quarters(near, near_0, 1, (1,))
     update_source([along(1), along(-1)])
+    pass_rims()
     (near_2,) = pass_quarters(near, near_1, 2, (1,))
     (far_3,) = pass_quarters(far, far_2, 3, (1,))
-    pass_rims()
     land(far_1)
     update_source([along(2), along(-2)])
     land(near_2)

time: 62.3 us -> 62.3 us (level)
  no operation moved by 1% of the time
where the time goes in v5:
time: 62.3 us; the launch traced here: 62.1 us
  Pallas kernels  60.8 us (98%)
  between operations  1.28 us (2%)
    pallas_call x1, Pallas kernels, local(): pl.pallas_call(functools.partial(fused_kernel, strips, float(shots * step...  59.1 us
    pallas_call x1, Pallas kernels, local(): pl.pallas_call(finish_kernel, out_shape=(upd, upd), in_specs=[VMEM, VMEM]...  1.78 us

profile of v5, /device:TPU:16, one launch (start us, length us, event | category | flops | bytes accessed | tf_op | source)
XLA Modules:
  0.0 62.1 jit_solution(4865083917940301361)
XLA Ops:
  1.3 59.1 %fused.1 = (f32[16,128,128]{2,1,0:T(8,128)S(1)}, f32[16,128,128]{2,1,0:T(8,128)S(1)}) custom-call(s32[1]{0:T(128)S(6)} %copy.6.shots_pos, bf16[16,8,16,128]{3,2,1,0:T(8,128)(2,1)} %bitcast.4, bf16[16,8,16,128]{3,2,1,0:T(8,128)(2,1)} %bitcast.5, s32[33]{0:T(128)} %weight_hbm.1), custom_call_target="tpu_custom_call" | custom-call | tf_op jit(solution)/shard_map/fused/pallas_call | solution.py:534
  60.4 1.8 %finish.1 = (f32[16,8,16,128]{3,2,1,0:T(8,128)}, f32[16,8,16,128]{3,2,1,0:T(8,128)}) custom-call(f32[16,128,128]{2,1,0:T(8,128)S(1)} %get-tuple-element.6.src_rows, f32[16,128,128]{2,1,0:T(8,128)S(1)} %get-tuple-element.7.rec_rows), custom_call_target="tpu_custom_call" | custom-call | tf_op jit(solution)/shard_map/finish/pallas_call | solution.py:574
